TPU v7x, 512 devices: a whole 4x8x8 slice. The times are simulated.
512 devices in a mesh: leaf: 128 (over z, y, core), rhs: 4 (over x).
Axes of the slice: x: 4, y: 8, z: 8, core: 2. Of those that a mesh axis runs over, the one named last changes fastest.
Arguments:
- leaf_shift: float32 [256, 262144], P('rhs', 'leaf'), may hold values from -6 to 6
- sep_shift: float32 [256, 4096], P('rhs', 'leaf'), may hold values from -6 to 6
- leaf_noise: float32 [256, 262144], P('rhs', 'leaf'), may hold values from -6 to 6
- sep_noise: float32 [256, 4096], P('rhs', 'leaf'), may hold values from -6 to 6
- leaf_inverse: float32 [2048, 128, 128], P('leaf'), may hold values from -1 to 2, as said below
- leaf_panel: float32 [2048, 64, 128], P('leaf'), may hold values from -0.0625 to 0.0625
- panel_blocks: int32 [2048, 8], P('leaf'), may hold values from 0 to 239, as said below
- sep_inverse: float32 [1024, 1920], P('leaf', 'rhs'), may hold values from -1 to 2, as said below
- sep_coupling: float32 [1024, 4352], P('leaf', 'rhs'), may hold values from -0.125 to 0.125
Outputs:
- leaf_sample: float32 [256, 262144], P('rhs', 'leaf')
- sep_sample: float32 [256, 4096], P('rhs', 'leaf')
Inputs may be any that keep to these rules, and one draw needn't show every extreme that they name: `leaf_inverse`: each [128, 128] block is lower triangular with a positive diagonal. `sep_inverse`: in the column block of depth k (columns O_k to O_k + S_k - 1), row p has zeros beyond column O_k + (p mod S_k) and a positive entry there: each separator's inverse is lower triangular. `panel_blocks`: the 8 numbers of a row are different.
All inputs are finite; a program needn't handle non-finite values.
Results may differ from a plain program's by a relative error of at most 0.00015.
Values sent between devices are 32-bit elements; how exact they have to be, the bound alone decides.
No kernel may reach another device: no remote copies, remote signals or barrier semaphores. Data moves between devices by JAX's collectives and lax.ppermute only.
A program may use at most 64 MiB of HBM per device.

v0:
```python
import jax
import jax.numpy as jnp
from jax import lax
from jax.sharding import PartitionSpec as P

SEP_DEV = 8
LEVELS = 4
NB = 8
exact_mode = lax.Precision.HIGHEST


def level_offsets(root_size):
    starts = [0]
    for height in range(LEVELS):
        starts.append(starts[-1] + (root_size >> height))
    return starts


def subcube_total(partial_value, height):
    leaf_count = lax.axis_size("leaf")
    dev_index = lax.axis_index("leaf")
    cube_size = leaf_count >> height
    sep_size = partial_value.shape[1]
    sep_start = dev_index // cube_size * sep_size
    buffer = jnp.zeros((partial_value.shape[0], SEP_DEV * leaf_count), jnp.float32)
    buffer = lax.dynamic_update_slice_in_dim(buffer, partial_value, sep_start, 1)
    summed = lax.psum(buffer, "leaf")
    full_sum = lax.dynamic_slice_in_dim(summed, sep_start, sep_size, 1)
    own_rows = lax.dynamic_slice_in_dim(full_sum, dev_index % cube_size * SEP_DEV, SEP_DEV, 1)
    return (own_rows, full_sum)


def body(
    leaf_shift,
    sep_shift,
    leaf_noise,
    sep_noise,
    leaf_inverse,
    leaf_panel,
    panel_blocks,
    sep_inverse,
    sep_coupling,
):
    inverse_rows, coupling_rows = (
        lax.all_gather(sep_inverse, "rhs", axis=1, tiled=True),
        lax.all_gather(sep_coupling, "rhs", axis=1, tiled=True),
    )
    leaf_count = lax.axis_size("leaf")
    dev_index = lax.axis_index("leaf")
    root_size = SEP_DEV * leaf_count
    starts = level_offsets(root_size)
    ancestry = starts[LEVELS]
    segment_at = [0]
    for height in range(1, LEVELS):
        segment_at.append(segment_at[-1] + starts[height])
    samples = leaf_shift.shape[0]
    node_count = leaf_inverse.shape[0]
    tile_size = leaf_inverse.shape[1]
    block_count = ancestry // SEP_DEV
    selector = (
        panel_blocks[:, :, None] == jnp.arange(block_count, dtype=jnp.int32)[None, None, :]
    ).astype(jnp.float32)
    shifted = leaf_shift.reshape(samples, node_count, tile_size)
    leaf_forward = jnp.einsum("rnt,nct->rnc", shifted, leaf_inverse, precision=exact_mode)
    pieces = jnp.einsum("rnc,nkc->rnk", leaf_forward, leaf_panel, precision=exact_mode)
    pieces = pieces.reshape(samples, node_count, NB, SEP_DEV)
    update = jnp.einsum("rnbi,nba->rai", pieces, selector, precision=exact_mode).reshape(
        samples, ancestry
    )
    sep_own = sep_shift.reshape(samples, LEVELS, SEP_DEV)
    noise_own = sep_noise.reshape(samples, LEVELS, SEP_DEV)
    forward_sep = [None] * LEVELS
    for height in reversed(range(LEVELS)):
        cube_size = leaf_count >> height
        sep_size = root_size >> height
        local_at = dev_index % cube_size * SEP_DEV
        placed = lax.dynamic_update_slice_in_dim(
            jnp.zeros((samples, sep_size), jnp.float32), sep_own[:, height, :], local_at, 1
        )
        partial_value = placed - update[:, starts[height] : starts[height] + sep_size]
        own_rows, full_rest = subcube_total(partial_value, height)
        inverse_block = inverse_rows[:, starts[height] : starts[height] + sep_size]
        solved = jnp.dot(full_rest, inverse_block.T, precision=exact_mode)
        forward_sep[height] = solved
        if height > 0:
            couple_block = coupling_rows[
                :, segment_at[height - 1] : segment_at[height - 1] + starts[height]
            ]
            update = update.at[:, : starts[height]].add(
                jnp.dot(solved, couple_block, precision=exact_mode)
            )
    gathered = jnp.zeros((samples, ancestry), jnp.float32)
    sep_result = [None] * LEVELS
    for height in range(LEVELS):
        sep_size = root_size >> height
        lifted = forward_sep[height] + noise_own[:, height, :]
        if height > 0:
            couple_block = coupling_rows[
                :, segment_at[height - 1] : segment_at[height - 1] + starts[height]
            ]
            lifted = lifted - jnp.dot(
                gathered[:, : starts[height]], couple_block.T, precision=exact_mode
            )
        inverse_block = inverse_rows[:, starts[height] : starts[height] + sep_size]
        partial_value = jnp.dot(lifted, inverse_block, precision=exact_mode)
        own_rows, full_sum = subcube_total(partial_value, height)
        sep_result[height] = own_rows
        gathered = lax.dynamic_update_slice_in_dim(gathered, full_sum, starts[height], 1)
    blocks_view = gathered.reshape(samples, block_count, SEP_DEV)
    picked = jnp.einsum("rai,nba->rnbi", blocks_view, selector, precision=exact_mode).reshape(
        samples, node_count, NB * SEP_DEV
    )
    leaf_lifted = leaf_forward + leaf_noise.reshape(samples, node_count, tile_size)
    leaf_lifted = leaf_lifted - jnp.einsum("rnk,nkc->rnc", picked, leaf_panel, precision=exact_mode)
    leaf_out = jnp.einsum("rnt,ntc->rnc", leaf_lifted, leaf_inverse, precision=exact_mode).reshape(
        samples, node_count * tile_size
    )
    sep_out = jnp.stack(sep_result, axis=1).reshape(samples, LEVELS * SEP_DEV)
    return (leaf_out, sep_out)


def solution(mesh):
    placed = (
        P("rhs", "leaf"),
        P("rhs", "leaf"),
        P("rhs", "leaf"),
        P("rhs", "leaf"),
        P("leaf", None, None),
        P("leaf", None, None),
        P("leaf", None),
        P("leaf", "rhs"),
        P("leaf", "rhs"),
    )
    return jax.shard_map(
        body,
        mesh=mesh,
        in_specs=placed,
        out_specs=(P("rhs", "leaf"), P("rhs", "leaf")),
        check_vma=False,
    )
```

profile of v0, /device:TPU:24, one launch (start us, length us, event | category | flops | bytes accessed | tf_op | source)
XLA Modules:
  0.0 1560.0 jit_solution(408747007953209379)
XLA Ops:
  7.3 0.8 copy-done.15
  8.0 0.1 copy.67
  8.1 0.3 copy-done
  8.4 3.2 convolution_bitcast_fusion.3
  11.6 1.0 convolution_bitcast_fusion.5
  12.6 1.0 copy.43
  13.7 1.6 convolution_bitcast_fusion.2
  15.3 0.4 copy.45
  15.8 0.4 dynamic_update_slice.45
  16.4 0.7 copy-done.6
  17.2 1.0 slice.157
  18.2 12.3 all-gather
  30.5 0.1 reshape.118
  30.7 12.0 all-gather.1
  42.7 0.1 reshape.120
  42.9 0.3 copy.66
  43.2 0.1 copy.69
  43.3 0.6 dynamic_update_slice.47
  43.9 0.6 compare_reduce_fusion
  44.5 167.7 %all-reduce.10.cloned.1.call-done = f32[64,1024]{1,0:T(8,128)} async-done(((f32[64,1024]{1,0:T(8,128)}), f32[64,1024]{1,0:T(8,128)}) %all-reduce.10.cloned.1.call-update) | async-done | bytes 262160 | tf_op jit(solution)/shard_map/psum | solution.py:27
  212.2 0.9 fusion.29
  213.1 1.2 fusion.1
  214.4 0.7 copy-done.7
  215.3 0.6 dynamic_update_slice.49
  215.9 0.6 compare_reduce_fusion.1
  216.6 186.1 %all-reduce.12.cloned.1.call-done = f32[64,1024]{1,0:T(8,128)} async-done(((f32[64,1024]{1,0:T(8,128)}), f32[64,1024]{1,0:T(8,128)}) %all-reduce.12.cloned.1.call-update) | async-done | bytes 262160 | tf_op jit(solution)/shard_map/psum | solution.py:27
  402.6 1.0 fusion.21
  403.6 1.2 fusion
  404.9 0.7 copy-done.8
  405.8 0.6 dynamic_update_slice.44
  406.4 0.6 compare_reduce_fusion.2
  407.0 186.0 %all-reduce.14.cloned.1.call-done = f32[64,1024]{1,0:T(8,128)} async-done(((f32[64,1024]{1,0:T(8,128)}), f32[64,1024]{1,0:T(8,128)}) %all-reduce.14.cloned.1.call-update) | async-done | bytes 262160 | tf_op jit(solution)/shard_map/psum | solution.py:27
  593.0 1.1 fusion.14
  594.1 1.8 fusion.4
  596.0 187.3 %all-reduce.16.cloned.1.call-done = f32[64,1024]{1,0:T(8,128)} async-done(((f32[64,1024]{1,0:T(8,128)}), f32[64,1024]{1,0:T(8,128)}) %all-reduce.16.cloned.1.call-update) | async-done | bytes 262160 | tf_op jit(solution)/shard_map/psum | solution.py:27
  783.3 1.2 convolution_add_fusion.3
  784.5 1.2 fusion.31
  785.8 187.8 %all-reduce.18.cloned.1.call-done = f32[64,1024]{1,0:T(8,128)} async-done(((f32[64,1024]{1,0:T(8,128)}), f32[64,1024]{1,0:T(8,128)}) %all-reduce.18.cloned.1.call-update) | async-done | bytes 262160 | tf_op jit(solution)/shard_map/psum | solution.py:27
  973.5 1.2 convolution_subtract_fusion
  974.8 0.3 convolution_dynamic-update-slice_fusion
  975.2 0.7 copy-done.9
  976.0 187.8 %all-reduce.20.cloned.1.call-done = f32[64,1024]{1,0:T(8,128)} async-done(((f32[64,1024]{1,0:T(8,128)}), f32[64,1024]{1,0:T(8,128)}) %all-reduce.20.cloned.1.call-update) | async-done | bytes 262160 | tf_op jit(solution)/shard_map/psum | solution.py:27
  1163.8 0.9 dynamic-slice_dynamic-update-slice_fusion
  1164.7 0.4 convolution_subtract_fusion.2
  1165.2 0.3 convolution_dynamic-update-slice_fusion.1
  1165.5 0.7 copy-done.10
  1166.2 0.2 all-reduce.24.cloned.1.call-start
  1166.6 187.6 %all-reduce.22.cloned.1.call-done = f32[64,1024]{1,0:T(8,128)} async-done(((f32[64,1024]{1,0:T(8,128)}), f32[64,1024]{1,0:T(8,128)}) %all-reduce.22.cloned.1.call-update) | async-done | bytes 262160 | tf_op jit(solution)/shard_map/psum | solution.py:27
  1354.2 0.8 dynamic-slice_dynamic-update-slice_fusion.1
  1355.1 0.5 convolution_subtract_fusion.1
  1355.6 0.2 convolution_dynamic-update-slice_fusion.2
  1355.8 0.7 copy-done.5
  1356.5 0.9 constant_dynamic-slice_fusion.1
  1357.5 0.9 constant_dynamic-slice_fusion
  1358.5 186.1 %all-reduce.24.cloned.1.call-done = f32[64,1024]{1,0:T(8,128)} async-done(((f32[64,1024]{1,0:T(8,128)}), f32[64,1024]{1,0:T(8,128)}) %all-reduce.24.cloned.1.call-update) | async-done | bytes 262160 | tf_op jit(solution)/shard_map/psum | solution.py:27
  1544.6 0.9 constant_dynamic-slice_fusion.3
  1545.6 0.8 dynamic-slice_dynamic-update-slice_fusion.2
  1546.4 0.3 copy.53
  1546.7 1.2 copy.54
  1547.9 1.7 convolution_bitcast_fusion.1
  1549.6 1.0 fusion.2
  1550.7 1.1 convolution_bitcast_fusion
  1551.7 0.8 copy.86
  1552.6 0.6 maximum_bitcast_fusion
  (68 shorter events, 1.5 us)
Async XLA Ops:
  7.2 1.2 copy-start
  7.2 205.0 %all-reduce.10.cloned.1.call-start = ((), (), s32[]{:S(2)}) async-start(), calls=%async_computation | async-start | bytes 524288 | tf_op jit(solution)/shard_map/psum | solution.py:27
  7.2 0.8 copy-start.15
  8.4 3.2 copy-start.2
  12.6 1.0 copy-start.16
  16.3 0.7 copy-start.6
  17.1 385.5 %all-reduce.12.cloned.1.call-start = ((), (), s32[]{:S(2)}) async-start(), calls=%async_computation.1 | async-start | bytes 524288 | tf_op jit(solution)/shard_map/psum | solution.py:27
  17.1 1.0 copy-start.14
  17.1 13.5 copy-start.12
  18.1 24.7 %copy-start.1 = (f32[64,1792]{0,1:T(8,128)S(1)}, f32[64,1792]{0,1:T(8,128)}, u32[]{:S(2)}) copy-start(f32[64,1792]{0,1:T(8,128)} %slice.157) | copy-start | bytes 1376260
  214.4 0.7 copy-start.7
  215.1 377.9 %all-reduce.14.cloned.1.call-start = ((), (), s32[]{:S(2)}) async-start(), calls=%async_computation.2 | async-start | bytes 524288 | tf_op jit(solution)/shard_map/psum | solution.py:27
  404.9 0.7 copy-start.8
  405.6 377.7 %all-reduce.16.cloned.1.call-start = ((), (), s32[]{:S(2)}) async-start(), calls=%async_computation.3 | async-start | bytes 524288 | tf_op jit(solution)/shard_map/psum | solution.py:27
  595.9 187.4 %copy-start.13 = (f32[64,32]{0,1:T(8,128)S(1)}, f32[64,32]{0,1:T(8,128)}, u32[]{:S(2)}) copy-start(f32[64,32]{0,1:T(8,128)} %param.18) | copy-start | bytes 24580
  595.9 377.6 %all-reduce.18.cloned.1.call-start = ((), (), s32[]{:S(2)}) async-start(), calls=%async_computation.4 | async-start | bytes 524288 | tf_op jit(solution)/shard_map/psum | solution.py:27
  785.7 378.1 %all-reduce.20.cloned.1.call-start = ((), (), s32[]{:S(2)}) async-start(), calls=%async_computation.5 | async-start | bytes 524288 | tf_op jit(solution)/shard_map/psum | solution.py:27
  974.8 1.1 copy-start.4
  975.2 0.7 copy-start.9
  975.9 378.3 %all-reduce.22.cloned.1.call-start = ((), (), s32[]{:S(2)}) async-start(), calls=%async_computation.6 | async-start | bytes 524288 | tf_op jit(solution)/shard_map/psum | solution.py:27
  1165.4 0.7 copy-start.10
  1166.2 378.4 %all-reduce.24.cloned.1.call-start = ((), (), s32[]{:S(2)}) async-start(), calls=%async_computation.7 | async-start | bytes 524288 | tf_op jit(solution)/shard_map/psum | solution.py:27
  1355.8 0.7 copy-start.5
  1547.9 1.7 copy-start.3
  1547.9 1.7 copy-start.11
Sparse Core Ops, SparseCore 0:
  17.2 194.9 all-reduce.9
  216.0 186.5 all-reduce.11
  406.4 186.5 all-reduce.13
  596.7 186.5 all-reduce.15
  786.9 186.5 all-reduce.17
  977.2 186.5 all-reduce.19
  1167.6 186.5 all-reduce.21
  1358.0 186.5 all-reduce.23
where the time goes:
time: 1560 us
  waiting for transfers between devices  1480 us (95%)
  blocking collectives  24.4 us (2%)
  matrix products  22.1 us (1%)
  local copies, waits for them, and re-layouts  19.3 us (1%)
    psum x8, waiting for transfers between devices, subcube_total(): summed = lax.psum(buffer, 'leaf')  1480 us
  transfers between devices with their start and end apart: 8, of which 8 were waited for; matrix products, arithmetic and copies ran while one was open for 0% of the time, Pallas kernels for 0%

commit v1 on v0

--- a/solution.py
+++ b/solution.py
@@ -24,7 +24,7 @@
     sep_start = dev_index // cube_size * sep_size
     buffer = jnp.zeros((partial_value.shape[0], SEP_DEV * leaf_count), jnp.float32)
     buffer = lax.dynamic_update_slice_in_dim(buffer, partial_value, sep_start, 1)
-    summed = lax.psum(buffer, "leaf")
+    summed = jnp.sum(lax.all_gather(buffer, "leaf"), axis=0)
     full_sum = lax.dynamic_slice_in_dim(summed, sep_start, sep_size, 1)
     own_rows = lax.dynamic_slice_in_dim(full_sum, dev_index % cube_size * SEP_DEV, SEP_DEV, 1)
     return (own_rows, full_sum)

time: 1560 us -> 1270 us (0.81)
  the two profiles are of different devices: /device:TPU:24 before, /device:TPU:1 now
where the time goes in v1:
time: 1270 us
  waiting for transfers between devices  1100 us (87%)
  other arithmetic  97.6 us (8%)
  blocking collectives  19.7 us (2%)
  matrix products  19.6 us (2%)
  local copies, waits for them, and re-layouts  17.3 us (1%)
  between operations  14.6 us (1%)
    all_gather x8, waiting for transfers between devices, subcube_total(): summed = jnp.sum(lax.all_gather(buffer, 'leaf'), axis=0)  1100 us
    reduce_sum x8, other arithmetic, subcube_total(): summed = jnp.sum(lax.all_gather(buffer, 'leaf'), axis=0)  95 us
  transfers between devices with their start and end apart: 8, of which 8 were waited for; matrix products, arithmetic and copies ran while one was open for 1% of the time, Pallas kernels for 0%

profile of v1, /device:TPU:1, one launch (start us, length us, event | category | flops | bytes accessed | tf_op | source)
XLA Modules:
  0.0 1265.9 jit_solution(5465781998571151356)
XLA Ops:
  7.2 1.1 copy-done
  8.4 3.1 convolution_bitcast_fusion.3
  11.6 2.0 convolution_bitcast_fusion.5
  13.5 0.2 copy.54
  13.8 0.8 copy.52
  14.5 1.4 convolution_bitcast_fusion.2
  15.9 1.4 copy.56
  17.4 0.7 constant_dynamic-update-slice_fusion.1
  18.2 0.7 copy-done.2
  19.0 1.0 slice.157
  20.0 10.4 all-gather.2
  30.5 9.4 all-gather.3
  39.9 0.1 reshape.134
  40.0 1.5 copy.76
  41.5 0.7 fusion.54
  42.3 0.6 dynamic_update_slice.53
  42.9 0.6 compare_reduce_fusion
  43.6 123.0 %all-gather.13.cloned.1.call-done = f32[128,64,1024]{2,1,0:T(8,128)} async-done(((f32[1,64,1024]{2,1,0:T(8,128)}), f32[128,64,1024]{2,1,0:T(8,128)}) %all-gather.13.cloned.1.call-update) | async-done | bytes 33554448 | tf_op jit(solution)/shard_map/all_gather | solution.py:27
  166.5 11.9 reduce_sum.72
  178.4 0.1 fusion.35
  178.6 1.2 fusion.1
  179.9 0.7 copy-done.3
  180.8 0.6 dynamic_update_slice.55
  181.4 0.6 compare_reduce_fusion.1
  182.0 138.2 %all-gather.15.cloned.1.call-done = f32[128,64,1024]{2,1,0:T(8,128)} async-done(((f32[1,64,1024]{2,1,0:T(8,128)}), f32[128,64,1024]{2,1,0:T(8,128)}) %all-gather.15.cloned.1.call-update) | async-done | bytes 33554448 | tf_op jit(solution)/shard_map/all_gather | solution.py:27
  320.2 11.9 reduce_sum.73
  332.1 0.2 fusion.27
  332.2 1.2 fusion
  333.5 0.7 copy-done.4
  334.4 0.6 dynamic_update_slice.50
  335.0 0.6 compare_reduce_fusion.2
  335.6 138.2 %all-gather.17.cloned.1.call-done = f32[128,64,1024]{2,1,0:T(8,128)} async-done(((f32[1,64,1024]{2,1,0:T(8,128)}), f32[128,64,1024]{2,1,0:T(8,128)}) %all-gather.17.cloned.1.call-update) | async-done | bytes 33554448 | tf_op jit(solution)/shard_map/all_gather | solution.py:27
  473.8 11.9 reduce_sum.74
  485.7 0.2 fusion.18
  485.9 1.8 fusion.4
  487.8 139.6 %all-gather.25.cloned.1.call-done = f32[8192,1024]{1,0:T(8,128)} async-done(((f32[64,1024]{1,0:T(8,128)}), f32[8192,1024]{1,0:T(8,128)}) %all-gather.25.cloned.1.call-update) | async-done | bytes 33554448 | tf_op jit(solution)/shard_map/all_gather | solution.py:27
  627.3 11.9 reduce_sum.75
  639.2 0.3 convolution_add_fusion.3
  639.5 1.2 fusion.37
  640.7 139.6 %all-gather.27.cloned.1.call-done = f32[8192,1024]{1,0:T(8,128)} async-done(((f32[64,1024]{1,0:T(8,128)}), f32[8192,1024]{1,0:T(8,128)}) %all-gather.27.cloned.1.call-update) | async-done | bytes 33554448 | tf_op jit(solution)/shard_map/all_gather | solution.py:27
  780.3 11.9 reduce_sum.76
  792.2 0.3 convolution_subtract_fusion
  792.5 0.3 fusion.5
  792.9 0.7 copy-done.5
  793.7 139.5 %all-gather.19.cloned.1.call-done = f32[128,64,1024]{2,1,0:T(8,128)} async-done(((f32[1,64,1024]{2,1,0:T(8,128)}), f32[128,64,1024]{2,1,0:T(8,128)}) %all-gather.19.cloned.1.call-update) | async-done | bytes 33554448 | tf_op jit(solution)/shard_map/all_gather | solution.py:27
  933.2 11.9 reduce_sum.77
  945.1 0.4 convolution_subtract_fusion.2
  945.5 0.3 fusion.6
  945.8 0.7 copy-done.6
  946.5 0.2 all-gather.23.cloned.1.call-start
  946.8 139.4 %all-gather.21.cloned.1.call-done = f32[128,64,1024]{2,1,0:T(8,128)} async-done(((f32[1,64,1024]{2,1,0:T(8,128)}), f32[128,64,1024]{2,1,0:T(8,128)}) %all-gather.21.cloned.1.call-update) | async-done | bytes 33554448 | tf_op jit(solution)/shard_map/all_gather | solution.py:27
  1086.1 11.9 reduce_sum.78
  1098.0 0.5 convolution_subtract_fusion.1
  1098.5 0.2 fusion.7
  1098.8 0.7 copy-done.1
  1100.0 139.1 %all-gather.23.cloned.1.call-done = f32[128,64,1024]{2,1,0:T(8,128)} async-done(((f32[1,64,1024]{2,1,0:T(8,128)}), f32[128,64,1024]{2,1,0:T(8,128)}) %all-gather.23.cloned.1.call-update) | async-done | bytes 33554448 | tf_op jit(solution)/shard_map/all_gather | solution.py:27
  1239.1 11.9 reduce_sum.79
  1251.2 0.3 copy.63
  1251.5 1.2 copy.64
  1252.7 1.6 convolution_bitcast_fusion.1
  1254.3 2.2 fusion.2
  1256.5 1.1 convolution_bitcast_fusion
  1257.6 0.8 copy.94
  1258.4 0.6 maximum_bitcast_fusion
  (57 shorter events, 1.9 us)
Async XLA Ops:
  7.2 1.2 copy-start
  7.2 159.4 %all-gather.13.cloned.1.call-start = ((), (), s32[]{:S(2)}) async-start(), calls=%async_computation | async-start | bytes 33816576 | tf_op jit(solution)/shard_map/all_gather | solution.py:27
  18.2 0.7 copy-start.2
  18.9 301.3 %all-gather.15.cloned.1.call-start = ((), (), s32[]{:S(2)}) async-start(), calls=%async_computation.1 | async-start | bytes 33816576 | tf_op jit(solution)/shard_map/all_gather | solution.py:27
  179.9 0.7 copy-start.3
  180.6 293.2 %all-gather.17.cloned.1.call-start = ((), (), s32[]{:S(2)}) async-start(), calls=%async_computation.2 | async-start | bytes 33816576 | tf_op jit(solution)/shard_map/all_gather | solution.py:27
  333.5 0.7 copy-start.4
  334.2 293.1 %all-gather.25.cloned.1.call-start = ((), (), s32[]{:S(2)}) async-start(), calls=%async_computation.6 | async-start | bytes 33816576 | tf_op jit(solution)/shard_map/all_gather | solution.py:27
  335.6 303.6 %copy-start.7 = (f32[64,32]{0,1:T(8,128)S(1)}, f32[64,32]{0,1:T(8,128)}, u32[]{:S(2)}) copy-start(f32[64,32]{0,1:T(8,128)} %param.18) | copy-start | bytes 24580
  487.7 292.6 %all-gather.27.cloned.1.call-start = ((), (), s32[]{:S(2)}) async-start(), calls=%async_computation.7 | async-start | bytes 33816576 | tf_op jit(solution)/shard_map/all_gather | solution.py:27
  640.7 292.5 %all-gather.19.cloned.1.call-start = ((), (), s32[]{:S(2)}) async-start(), calls=%async_computation.3 | async-start | bytes 33816576 | tf_op jit(solution)/shard_map/all_gather | solution.py:27
  792.8 0.7 copy-start.5
  793.6 292.6 %all-gather.21.cloned.1.call-start = ((), (), s32[]{:S(2)}) async-start(), calls=%async_computation.4 | async-start | bytes 33816576 | tf_op jit(solution)/shard_map/all_gather | solution.py:27
  945.8 0.7 copy-start.6
  946.5 292.6 %all-gather.23.cloned.1.call-start = ((), (), s32[]{:S(2)}) async-start(), calls=%async_computation.5 | async-start | bytes 33816576 | tf_op jit(solution)/shard_map/all_gather | solution.py:27
  1098.8 0.7 copy-start.1
Sparse Core Ops, SparseCore 0:
  19.1 147.4 all-gather.12
  180.7 139.4 all-gather.14
  334.3 139.4 all-gather.16
  487.9 139.4 all-gather.24
  640.8 139.4 all-gather.26
  793.7 139.4 all-gather.18
  946.7 139.4 all-gather.20
  1099.6 139.4 all-gather.22
